TPU v7x, 512 devices: a whole 4x4x16 slice. The times are simulated.
512 devices in a mesh: member: 8 (over y, x_hi), space: 64 (over x_lo, z, core).
Axes of the slice: x: 4 (x_hi: 2, x_lo: 2; x = x_hi * 2 + x_lo), y: 4, z: 16, core: 2. Of those that a mesh axis runs over, the one named last changes fastest.
Arguments:
- latent: bfloat16 [16, 4096, 1024], P('member', 'space'), may hold values from -6 to 6
- edge_weight: float32 [3, 32768], P(None, 'space'), may hold values from 0.1 to 1
- neighbours: int32 [3, 32768], P(None, 'space'), may hold values from 0 to 4095, as said below
- band_rows: int32 [64], P('space'), may hold values from 1 to 512, 24576 in all
- w_in: bfloat16 [1024, 1024], replicated, may hold values from -0.1875 to 0.1875
- w_out: bfloat16 [69, 1024], replicated, may hold values from -0.1875 to 0.1875
- target: float32 [69, 32768], P(None, 'space'), may hold values from -80 to 80
Outputs:
- score: float32 [], replicated
- grad_latent: bfloat16 [16, 4096, 1024], P('member', 'space')
- grad_w_out: float32 [69, 1024], P(None, 'space')
Inputs may be any that keep to these rules, and one draw needn't show every extreme that they name: `neighbours`: the node of an edge at grid slot g lies in latitude band g // 512 or one of the two bands beside it, node band b holding nodes b * 64 to (b + 1) * 64 - 1. Band b holds real grid points in its first band_rows[b] slots and padding after them; some band is full.
All inputs are finite; a program needn't handle non-finite values. No bound on the sum of `band_rows` on one device may be relied on, other than what follows from the above.
Results may differ from a plain program's by a relative error of at most 0.0075.
Values may be sent and summed in bfloat16 or wider, within the bound.
No kernel may reach another device: no remote copies, remote signals or barrier semaphores. Data moves between devices by JAX's collectives and lax.ppermute only.
A program may use at most 64 MiB of HBM per device.

v0:
```python
import jax
import jax.numpy as jnp
from jax import lax
from jax.sharding import PartitionSpec as P

epsilon = 1e-06


def extended_2(array, sides, width):
    for axis, dim in sides:
        size, length = (lax.axis_size(axis), array.shape[dim])
        up = [(i, (i + 1) % size) for i in range(size - 1)]
        down = [(j, i) for i, j in up]
        last = lax.slice_in_dim(array, length - width, length, axis=dim)
        first = lax.slice_in_dim(array, 0, width, axis=dim)
        before = lax.ppermute(last, axis, up)
        after = lax.ppermute(first, axis, down)
        array = jnp.concatenate([before, array, after], axis=dim)
    return array


def passed_along(array, axis, by):
    length = lax.axis_size(axis)
    pairs = [(i, i + by) for i in range(length) if 0 <= i + by < length]
    return lax.ppermute(array, axis, pairs)


def partials(everyone, target_rows, valid_rows):
    deviation = everyone - target_rows[None]
    target_sums = jnp.sum(valid_rows * deviation * deviation, axis=(1, 2))

    def against(member_field):
        spread = everyone - member_field[None]
        return jnp.sum(valid_rows * spread * spread, axis=(1, 2))

    pair_sums = lax.map(against, everyone)
    return (target_sums, pair_sums, jnp.sum(valid_rows))


def finish(target_sums, pair_sums, cell_count, variables):
    members = target_sums.shape[0]
    cells = variables * cell_count
    target_dist = jnp.sqrt(target_sums / cells + epsilon)
    pair_dist = jnp.sqrt(pair_sums / cells + epsilon)
    apart = 1.0 - jnp.eye(members, dtype=jnp.float32)
    pair_coef = apart / pair_dist
    score = jnp.mean(target_dist) - jnp.sum(apart * pair_dist) / (2.0 * members * (members - 1))
    return (score, pair_coef, target_dist)


def member_grads(chosen, everyone, coef_rows, dist_rows, target_rows, valid_rows):
    members = everyone.shape[0]
    others = jnp.sum(coef_rows[:, :, None, None] * everyone[None], axis=1)
    spread = jnp.sum(coef_rows, axis=1)[:, None, None] * chosen - others
    toward = (chosen - target_rows[None]) / (members * dist_rows[:, None, None])
    return (valid_rows * (toward - spread / (members * (members - 1)))).astype(jnp.bfloat16)


def per_device(latent, edge_weight, neighbours, band_rows, w_in, w_out, target):
    members_dev, nodes_dev, latent_width = latent.shape
    neigh_count, row_count = edge_weight.shape
    variables = w_out.shape[0]
    band_index = lax.axis_index("space")
    extended = extended_2(latent, (("space", 1),), nodes_dev)
    local_index = neighbours - (band_index - 1) * nodes_dev
    picked = jnp.take(extended, local_index.reshape(-1), axis=1).reshape(
        members_dev, neigh_count, row_count, latent_width
    )
    aggregated = edge_weight[0][None, :, None] * picked[:, 0].astype(jnp.float32)
    for neighbour in range(1, neigh_count):
        aggregated = aggregated + edge_weight[neighbour][None, :, None] * picked[
            :, neighbour
        ].astype(jnp.float32)
    latent_mix = aggregated.astype(jnp.bfloat16)
    preact = jnp.einsum("mgd,de->mge", latent_mix, w_in, preferred_element_type=jnp.float32)
    hidden = jax.nn.silu(preact).astype(jnp.bfloat16)
    fields = jnp.einsum("vd,mgd->mvg", w_out, hidden, preferred_element_type=jnp.float32).astype(
        jnp.bfloat16
    )
    valid_rows = (jnp.arange(row_count) < band_rows[0]).astype(jnp.float32)
    everyone = lax.all_gather(fields, "member", axis=0, tiled=True).astype(jnp.float32)
    target_sums, pair_sums, cell_count = partials(everyone, target, valid_rows)
    target_sums, pair_sums, cell_count = lax.psum((target_sums, pair_sums, cell_count), "space")
    score, pair_coef, target_dist = finish(target_sums, pair_sums, cell_count, variables)
    first_member = lax.axis_index("member") * members_dev
    coef_rows = lax.dynamic_slice_in_dim(pair_coef, first_member, members_dev, 0)
    dist_rows = lax.dynamic_slice_in_dim(target_dist, first_member, members_dev, 0)
    grad_fields = member_grads(
        fields.astype(jnp.float32), everyone, coef_rows, dist_rows, target, valid_rows
    )
    partial_weight = jnp.einsum(
        "mvg,mgd->vd", grad_fields, hidden, preferred_element_type=jnp.float32
    )
    summed = lax.psum(partial_weight, ("member", "space"))
    column_count = latent_width // lax.axis_size("space")
    grad_w_out = lax.dynamic_slice_in_dim(summed, band_index * column_count, column_count, 1)
    back = jnp.einsum("vd,mvg->mgd", w_out, grad_fields, preferred_element_type=jnp.float32)
    sigmoid_part = jax.nn.sigmoid(preact)
    grad_pre = (back * sigmoid_part * (1.0 + preact * (1.0 - sigmoid_part))).astype(jnp.bfloat16)
    grad_mixed = jnp.einsum("mge,de->mgd", grad_pre, w_in, preferred_element_type=jnp.float32)
    spread_terms = (edge_weight[None, :, :, None] * grad_mixed[:, None]).reshape(
        members_dev, -1, latent_width
    )
    flat_index = local_index.reshape(-1)
    collected = jax.vmap(
        lambda edge_terms: jax.ops.segment_sum(edge_terms, flat_index, num_segments=3 * nodes_dev)
    )(spread_terms)
    lower_rim = collected[:, :nodes_dev].astype(jnp.bfloat16)
    middle_rows = collected[:, nodes_dev : 2 * nodes_dev]
    upper_rim = collected[:, 2 * nodes_dev :].astype(jnp.bfloat16)
    from_above = passed_along(lower_rim, "space", -1)
    from_below = passed_along(upper_rim, "space", 1)
    grad_latent = (
        middle_rows + from_above.astype(jnp.float32) + from_below.astype(jnp.float32)
    ).astype(jnp.bfloat16)
    return (score, grad_latent, grad_w_out)


def solution(mesh):
    return jax.shard_map(
        per_device,
        mesh=mesh,
        in_specs=(
            P("member", "space", None),
            P(None, "space"),
            P(None, "space"),
            P("space"),
            P(),
            P(),
            P(None, "space"),
        ),
        out_specs=(P(), P("member", "space", None), P(None, "space")),
        check_vma=False,
    )
```

profile of v0, /device:TPU:4, one launch (start us, length us, event | category | flops | bytes accessed | tf_op | source)
XLA Modules:
  0.0 1032.3 jit_solution(2826235210925329485)
XLA Ops:
  7.2 1.4 copy.28
  8.6 1.8 collective-permute-start
  10.4 1.3 collective-permute-start.1
  11.7 0.7 compare_and_fusion
  12.4 0.8 fusion.35
  13.2 2.4 collective-permute-done.1
  15.6 2.0 pad_maximum_fusion
  17.6 41.8 %gather_fusion = bf16[1536,2,1024]{2,1,0:T(2,128)(2,1)} fusion(bf16[2,192,1024]{2,0,1:T(2,128)(2,1)S(1)} %pad_maximum_fusion, s32[2048]{0:T(1024)S(1)} %pad_clamp_fusion), kind=kCustom, calls=%fused_computation | custom fusion | bytes 12589056 | tf_op jit(solution)/shard_map/jit(_take)/gather | solution.py:66
  59.5 6.4 copy_select_fusion
  65.9 4.7 multiply_convert_fusion.1
  70.6 1.4 copy-done.2
  72.0 1.4 fusion.16
  75.0 67.4 %all-gather.2.cloned.1.call-done = bf16[16,69,512]{2,1,0:T(8,128)(2,1)} async-done(((bf16[2,69,512]{2,1,0:T(8,128)(2,1)}), bf16[16,69,512]{2,1,0:T(8,128)(2,1)}) %all-gather.2.cloned.1.call-update) | async-done | bytes 1130512 | tf_op jit(solution)/shard_map/all_gather | solution.py:81
  142.3 3.0 convert_element_type.76
  145.4 59.9 %while.11 = (s32[]{:T(128)}, f32[16,16]{1,0:T(8,128)S(1)}, f32[16,69,512]{2,1,0:T(8,128)}, s32[]{:T(128)}, s32[]{:T(128)}, /*index=5*/s32[]{:T(128)}) while((s32[]{:T(128)}, f32[16,16]{1,0:T(8,128)S(1)}, f32[16,69,512]{2,1,0:T(8,128)}, s32[]{:T(128)}, s32[]{:T(128)}, /*index=5*/s32[]{:T(128)}) %tuple.38), condition=%wide.region_7.8_spmd.clone, body=%wide.region_5.7_spmd.clone.sunk | while | flops 2262002 | bytes 2689297 | solution.py:36
  145.4 1.0 dynamic-slice_bitcast_fusion.2
  147.0 2.1 fusion.44
  149.2 0.9 dynamic-slice_bitcast_fusion.2
  150.8 2.1 fusion.44
  152.9 0.9 dynamic-slice_bitcast_fusion.2
  154.5 2.1 fusion.44
  156.7 0.9 dynamic-slice_bitcast_fusion.2
  158.2 2.1 fusion.44
  160.4 0.9 dynamic-slice_bitcast_fusion.2
  162.0 2.1 fusion.44
  164.1 0.9 dynamic-slice_bitcast_fusion.2
  165.7 2.1 fusion.44
  167.9 0.9 dynamic-slice_bitcast_fusion.2
  169.5 2.1 fusion.44
  171.6 0.9 dynamic-slice_bitcast_fusion.2
  173.2 2.1 fusion.44
  175.4 0.9 dynamic-slice_bitcast_fusion.2
  176.9 2.1 fusion.44
  179.1 0.9 dynamic-slice_bitcast_fusion.2
  180.7 2.1 fusion.44
  182.8 0.9 dynamic-slice_bitcast_fusion.2
  184.4 2.1 fusion.44
  186.6 0.9 dynamic-slice_bitcast_fusion.2
  188.2 2.1 fusion.44
  190.3 0.9 dynamic-slice_bitcast_fusion.2
  191.9 2.1 fusion.44
  194.0 0.9 dynamic-slice_bitcast_fusion.2
  195.6 2.1 fusion.44
  197.8 0.9 dynamic-slice_bitcast_fusion.2
  199.4 2.1 fusion.44
  201.5 0.9 dynamic-slice_bitcast_fusion.2
  203.1 2.1 fusion.44
  205.3 1.5 fusion.7
  206.7 112.9 %all-reduce = (f32[16]{0:T(128)S(1)}, f32[]{:T(128)}, f32[16,16]{1,0:T(8,128)S(1)}) all-reduce(f32[16]{0:T(128)S(1)} %fusion.7, f32[]{:T(128)} %fusion.30, f32[16,16]{1,0:T(8,128)S(1)} %get-tuple-element.25), channel_id=1, replica_groups=mesh['member'=8,'space'=64] {'space'}, use_global_device_ids=true, to_apply=%region_1.2 | all-reduce | flops 273 | bytes 2184 | tf_op jit(solution)/shard_map/psum | solution.py:83
  322.1 1.1 multiply_reduce_fusion
  323.2 7.9 fusion.10
  331.1 5.4 copy.33
  336.5 10.1 bitcast_multiply_fusion
  346.6 1.6 broadcast_in_dim.23
  348.2 211.3 %scatter_fusion = f32[2,192,1024]{2,0,1:T(2,128)} fusion(f32[2,192,1024]{2,0,1:T(2,128)} %broadcast_in_dim.23, s32[1536]{0:T(1024)S(1)} %reshape.87, f32[1536,2,1024]{2,1,0:T(2,128)} %bitcast.66), kind=kCustom, calls=%fused_computation.1 | custom fusion | flops 3145728 | bytes 37754880 | tf_op jit(solution)/shard_map/vmap()/scatter-add | solution.py:106
  559.5 1.9 convert.7
  561.4 1.1 fusion.34
  562.5 1.3 collective-permute-start.2
  563.8 3.0 collective-permute-start.3
  566.9 3.4 convolution_bitcast_fusion
  571.6 449.3 %all-reduce.3.cloned.1.call-done = f32[69,1024]{0,1:T(8,128)} async-done(((f32[69,1024]{0,1:T(8,128)}), f32[69,1024]{0,1:T(8,128)}) %all-reduce.3.cloned.1.call-update) | async-done | bytes 282640 | tf_op jit(solution)/shard_map/psum | solution.py:94
  1020.9 1.3 constant_dynamic-slice_fusion
  1022.2 1.4 fusion.18
  1023.6 0.8 copy.35
  (63 shorter events, 13.6 us)
Async XLA Ops:
  7.2 58.7 %copy-start = (bf16[1024,1024]{1,0:T(8,128)(2,1)S(1)}, bf16[1024,1024]{1,0:T(8,128)(2,1)}, u32[]{:S(2)}) copy-start(bf16[1024,1024]{1,0:T(8,128)(2,1)} %param.13) | copy-start | bytes 6291460
  7.2 135.2 %all-gather.2.cloned.1.call-start = ((), (), s32[]{:S(2)}) async-start(), calls=%async_computation | async-start | bytes 1327104 | tf_op jit(solution)/shard_map/all_gather | solution.py:81
  8.6 4.7 collective-permute-start
  10.4 5.3 collective-permute-start.1
  65.9 6.1 copy-start.4
  65.9 7.8 copy-start.5
  70.6 1.4 copy-start.2
  73.4 947.4 %all-reduce.3.cloned.1.call-start = ((), (), s32[]{:S(2)}) async-start(), calls=%async_computation.1 | async-start | bytes 1048576 | tf_op jit(solution)/shard_map/psum | solution.py:94
  145.4 59.9 %copy-start.1 = (bf16[16,69,512]{2,1,0:T(8,128)(2,1)S(1)}, bf16[16,69,512]{2,1,0:T(8,128)(2,1)}, u32[]{:S(2)}) copy-start(bf16[16,69,512]{2,1,0:T(8,128)(2,1)} %all-gather.2.cloned.1.call-done) | copy-start | bytes 3391492
  205.3 117.9 %copy-start.3 = (bf16[2,69,512]{2,1,0:T(8,128)(2,1)S(1)}, bf16[2,69,512]{2,1,0:T(8,128)(2,1)}, u32[]{:S(2)}) copy-start(bf16[2,69,512]{2,1,0:T(8,128)(2,1)} %fusion.16) | copy-start | bytes 423940
  562.5 459.7 %collective-permute-start.2 = (bf16[2,64,1024]{2,0,1:T(2,128)(2,1)}, bf16[2,64,1024]{2,0,1:T(2,128)(2,1)S(1)}, u32[]{:S(2)}, u32[]{:S(2)}) collective-permute-start(bf16[2,64,1024]{2,0,1:T(2,128)(2,1)} %get-tuple-element.68), channel_id=1, source_target_pairs={{1,0},{2,1},{3,2},{4,3},{5,4},{6,5},{7,6},{8,7},{9,8},{10,9},{11,1... | collective-permute-start | bytes 786440 | tf_op jit(solution)/shard_map/ppermute | solution.py:25
  563.8 458.4 %collective-permute-start.3 = (bf16[2,64,1024]{2,0,1:T(2,128)(2,1)S(1)}, bf16[2,64,1024]{2,0,1:T(2,128)(2,1)S(1)}, u32[]{:S(2)}, u32[]{:S(2)}) collective-permute-start(bf16[2,64,1024]{2,0,1:T(2,128)(2,1)S(1)} %get-tuple-element.69), channel_id=1, source_target_pairs={{0,1},{1,2},{2,3},{3,4},{4,5},{5,6},{6,7},{7,8},{8,9},{9,10},{10,1... | collective-permute-start | bytes 786440 | tf_op jit(solution)/shard_map/ppermute | solution.py:25
Sparse Core Ops, SparseCore 0:
  73.6 68.7 all-gather.1
  570.4 450.4 all-reduce.2
where the time goes:
time: 1040 us; the launch traced here: 1030 us
  waiting for transfers between devices  519 us (50%)
  other arithmetic  286 us (28%)
  blocking collectives  113 us (11%)
  local copies, waits for them, and re-layouts  71.2 us (7%)
  between operations  18 us (2%)
  matrix products  17.5 us (2%)
    psum x1, waiting for transfers between devices, per_device(): summed = lax.psum(partial_weight, ('member', 'space'))  449 us
    scatter-add x1, other arithmetic, per_device(): jax.ops.segment_sum(edge_terms, flat_index, num_segments=3 * nodes_dev)  211 us
    psum x1, blocking collectives, per_device(): lax.psum((target_sums, pair_sums, cell_count), 'space')  113 us
    all_gather x1, waiting for transfers between devices, per_device(): lax.all_gather(fields, 'member', axis=0, tiled=True).astype(jnp.float32)  67.4 us
    gather x1, local copies, waits for them, and re-layouts, per_device(): jnp.take(extended, local_index.reshape(-1), axis=1)  41.8 us
    reduce_sum x16, other arithmetic, against(): return jnp.sum(valid_rows * spread * spread, axis=(1, 2))  33.9 us
  transfers between devices with their start and end apart: 6, of which 3 were waited for; matrix products, arithmetic and copies ran while one was open for 1% of the time, Pallas kernels for 0%

commit v1 on v0

--- a/solution.py
+++ b/solution.py
@@ -91,7 +91,7 @@
     partial_weight = jnp.einsum(
         "mvg,mgd->vd", grad_fields, hidden, preferred_element_type=jnp.float32
     )
-    summed = lax.psum(partial_weight, ("member", "space"))
+    summed = lax.psum(lax.psum(partial_weight, "member"), "space")
     column_count = latent_width // lax.axis_size("space")
     grad_w_out = lax.dynamic_slice_in_dim(summed, band_index * column_count, column_count, 1)
     back = jnp.einsum("vd,mvg->mgd", w_out, grad_fields, preferred_element_type=jnp.float32)

time: 1040 us -> 1000 us (0.962)
  the two profiles are of different devices: /device:TPU:4 before, /device:TPU:1 now
where the time goes in v1:
time: 1000 us; the launch traced here: 998 us
  waiting for transfers between devices  480 us (48%)
  other arithmetic  286 us (29%)
  blocking collectives  111 us (11%)
  local copies, waits for them, and re-layouts  70.5 us (7%)
  between operations  17.8 us (2%)
  starting transfers between devices  16.7 us (2%)
  matrix products  15.7 us (2%)
    psum x2, waiting for transfers between devices, per_device(): summed = lax.psum(lax.psum(partial_weight, 'member'), 'space')  413 us
    scatter-add x1, other arithmetic, per_device(): jax.ops.segment_sum(edge_terms, flat_index, num_segments=3 * nodes_dev)  211 us
    psum x1, blocking collectives, per_device(): lax.psum((target_sums, pair_sums, cell_count), 'space')  111 us
    all_gather x1, waiting for transfers between devices, per_device(): lax.all_gather(fields, 'member', axis=0, tiled=True).astype(jnp.float32)  63.6 us
    gather x1, local copies, waits for them, and re-layouts, per_device(): jnp.take(extended, local_index.reshape(-1), axis=1)  41.8 us
    reduce_sum x16, other arithmetic, against(): return jnp.sum(valid_rows * spread * spread, axis=(1, 2))  33.9 us
  transfers between devices with their start and end apart: 7, of which 4 were waited for; matrix products, arithmetic and copies ran while one was open for 24% of the time, Pallas kernels for 0%

profile of v1, /device:TPU:1, one launch (start us, length us, event | category | flops | bytes accessed | tf_op | source)
XLA Modules:
  0.0 997.6 jit_solution(17609380679279575429)
XLA Ops:
  7.2 1.4 copy.28
  8.6 4.9 collective-permute-start
  13.5 5.2 collective-permute-start.1
  18.7 0.7 compare_and_fusion
  19.5 0.8 fusion.35
  20.3 1.0 collective-permute-done.1
  21.3 2.0 pad_maximum_fusion
  23.4 41.8 %gather_fusion = bf16[1536,2,1024]{2,1,0:T(2,128)(2,1)} fusion(bf16[2,192,1024]{2,0,1:T(2,128)(2,1)S(1)} %pad_maximum_fusion, s32[2048]{0:T(1024)S(1)} %pad_clamp_fusion), kind=kCustom, calls=%fused_computation | custom fusion | bytes 12589056 | tf_op jit(solution)/shard_map/jit(_take)/gather | solution.py:66
  65.2 6.4 copy_select_fusion
  71.6 4.7 multiply_convert_fusion.1
  76.4 1.3 copy-done.2
  77.7 1.4 fusion.16
  80.7 63.6 %all-gather.2.cloned.1.call-done = bf16[16,69,512]{2,1,0:T(8,128)(2,1)} async-done(((bf16[2,69,512]{2,1,0:T(8,128)(2,1)}), bf16[16,69,512]{2,1,0:T(8,128)(2,1)}) %all-gather.2.cloned.1.call-update) | async-done | bytes 1130512 | tf_op jit(solution)/shard_map/all_gather | solution.py:81
  144.3 3.0 convert_element_type.76
  147.3 59.9 %while.11 = (s32[]{:T(128)}, f32[16,16]{1,0:T(8,128)S(1)}, f32[16,69,512]{2,1,0:T(8,128)}, s32[]{:T(128)}, s32[]{:T(128)}, /*index=5*/s32[]{:T(128)}) while((s32[]{:T(128)}, f32[16,16]{1,0:T(8,128)S(1)}, f32[16,69,512]{2,1,0:T(8,128)}, s32[]{:T(128)}, s32[]{:T(128)}, /*index=5*/s32[]{:T(128)}) %tuple.38), condition=%wide.region_7.8_spmd.clone, body=%wide.region_5.7_spmd.clone.sunk | while | flops 2262002 | bytes 2689297 | solution.py:36
  147.3 1.0 dynamic-slice_bitcast_fusion.2
  149.0 2.1 fusion.44
  151.1 0.9 dynamic-slice_bitcast_fusion.2
  152.7 2.1 fusion.44
  154.9 0.9 dynamic-slice_bitcast_fusion.2
  156.5 2.1 fusion.44
  158.6 0.9 dynamic-slice_bitcast_fusion.2
  160.2 2.1 fusion.44
  162.4 0.9 dynamic-slice_bitcast_fusion.2
  163.9 2.1 fusion.44
  166.1 0.9 dynamic-slice_bitcast_fusion.2
  167.7 2.1 fusion.44
  169.8 0.9 dynamic-slice_bitcast_fusion.2
  171.4 2.1 fusion.44
  173.6 0.9 dynamic-slice_bitcast_fusion.2
  175.2 2.1 fusion.44
  177.3 0.9 dynamic-slice_bitcast_fusion.2
  178.9 2.1 fusion.44
  181.0 0.9 dynamic-slice_bitcast_fusion.2
  182.6 2.1 fusion.44
  184.8 0.9 dynamic-slice_bitcast_fusion.2
  186.4 2.1 fusion.44
  188.5 0.9 dynamic-slice_bitcast_fusion.2
  190.1 2.1 fusion.44
  192.3 0.9 dynamic-slice_bitcast_fusion.2
  193.8 2.1 fusion.44
  196.0 0.9 dynamic-slice_bitcast_fusion.2
  197.6 2.1 fusion.44
  199.7 0.9 dynamic-slice_bitcast_fusion.2
  201.3 2.1 fusion.44
  203.5 0.9 dynamic-slice_bitcast_fusion.2
  205.1 2.1 fusion.44
  207.2 1.5 fusion.7
  208.7 110.8 %all-reduce = (f32[16]{0:T(128)S(1)}, f32[]{:T(128)}, f32[16,16]{1,0:T(8,128)S(1)}) all-reduce(f32[16]{0:T(128)S(1)} %fusion.7, f32[]{:T(128)} %fusion.30, f32[16,16]{1,0:T(8,128)S(1)} %get-tuple-element.25), channel_id=1, replica_groups=mesh['member'=8,'space'=64] {'space'}, use_global_device_ids=true, to_apply=%region_1.2 | all-reduce | flops 273 | bytes 2184 | tf_op jit(solution)/shard_map/psum | solution.py:83
  322.0 1.1 multiply_reduce_fusion
  323.1 1.8 convolution_bitcast_fusion
  325.0 7.7 fusion.10
  332.8 5.4 copy.33
  338.2 10.1 %bitcast_multiply_fusion = f32[2,1536,1024]{2,0,1:T(2,128)} fusion(f32[1536]{0:T(1024)S(1)} %mul.143, f32[2,512,1024]{2,0,1:T(2,128)S(1)} %copy.33), kind=kLoop, calls=%fused_computation.8 | loop fusion | flops 3145728 | bytes 16783360 | tf_op jit(solution)/shard_map/mul | solution.py:101
  348.3 1.6 broadcast_in_dim.23
  349.9 211.4 %scatter_fusion = f32[2,192,1024]{2,0,1:T(2,128)} fusion(f32[2,192,1024]{2,0,1:T(2,128)} %broadcast_in_dim.23, s32[1536]{0:T(1024)S(1)} %reshape.87, f32[1536,2,1024]{2,1,0:T(2,128)} %bitcast.66), kind=kCustom, calls=%fused_computation.1 | custom fusion | flops 3145728 | bytes 37754880 | tf_op jit(solution)/shard_map/vmap()/scatter-add | solution.py:106
  561.3 1.9 convert.7
  563.6 4.4 collective-permute-start.2
  568.0 1.9 collective-permute-start.3
  571.3 1.9 collective-permute-done.3
  573.2 1.4 fusion.18
  574.6 0.8 copy.35
  575.4 413.2 %all-reduce.6.cloned.1.call-done = f32[69,1024]{0,1:T(8,128)} async-done(((f32[69,1024]{0,1:T(8,128)}), f32[69,1024]{0,1:T(8,128)}) %all-reduce.6.cloned.1.call-update) | async-done | bytes 282640 | tf_op jit(solution)/shard_map/psum | solution.py:94
  988.6 1.3 constant_dynamic-slice_fusion
  (74 shorter events, 14.1 us)
Async XLA Ops:
  7.2 64.4 %copy-start = (bf16[1024,1024]{1,0:T(8,128)(2,1)S(1)}, bf16[1024,1024]{1,0:T(8,128)(2,1)}, u32[]{:S(2)}) copy-start(bf16[1024,1024]{1,0:T(8,128)(2,1)} %param.13) | copy-start | bytes 6291460
  7.2 137.1 %all-gather.2.cloned.1.call-start = ((), (), s32[]{:S(2)}) async-start(), calls=%async_computation | async-start | bytes 1327104 | tf_op jit(solution)/shard_map/all_gather | solution.py:81
  8.6 11.7 %collective-permute-start = (bf16[2,64,1024]{2,0,1:T(2,128)(2,1)S(1)}, bf16[2,64,1024]{2,0,1:T(2,128)(2,1)S(1)}, u32[]{:S(2)}, u32[]{:S(2)}) collective-permute-start(bf16[2,64,1024]{2,0,1:T(2,128)(2,1)S(1)} %copy.28), channel_id=1, source_target_pairs={{0,1},{1,2},{2,3},{3,4},{4,5},{5,6},{6,7},{7,8},{8,9},{9,10},{10,1... | collective-permute-start | bytes 786440 | tf_op jit(solution)/shard_map/ppermute | solution.py:16
  13.5 7.8 collective-permute-start.1
  71.6 6.1 copy-start.7
  71.6 7.8 copy-start.9
  76.4 1.3 copy-start.2
  79.2 490.8 %all-reduce.4.cloned.1.call-start = ((), (), s32[]{:S(2)}) async-start(), calls=%async_computation.1 | async-start | bytes 1048576 | tf_op jit(solution)/shard_map/psum | solution.py:94
  147.3 59.9 %copy-start.1 = (bf16[16,69,512]{2,1,0:T(8,128)(2,1)S(1)}, bf16[16,69,512]{2,1,0:T(8,128)(2,1)}, u32[]{:S(2)}) copy-start(bf16[16,69,512]{2,1,0:T(8,128)(2,1)} %all-gather.2.cloned.1.call-done) | copy-start | bytes 3391492
  207.2 115.9 %copy-start.4 = (bf16[2,69,512]{2,1,0:T(8,128)(2,1)S(1)}, bf16[2,69,512]{2,1,0:T(8,128)(2,1)}, u32[]{:S(2)}) copy-start(bf16[2,69,512]{2,1,0:T(8,128)(2,1)} %fusion.16) | copy-start | bytes 423940
  320.2 2.9 copy-start.3
  320.2 2.9 copy-start.5
  322.0 3.0 copy-start.6
  322.0 3.0 copy-start.8
  325.0 663.6 %all-reduce.6.cloned.1.call-start = ((), (), s32[]{:S(2)}) async-start(), calls=%async_computation.2 | async-start | bytes 1048576 | tf_op jit(solution)/shard_map/psum | solution.py:94
  563.6 7.7 collective-permute-start.2
  568.0 5.2 collective-permute-start.3
Sparse Core Ops, SparseCore 0:
  79.3 64.9 all-gather.1
  325.1 87.2 all-reduce.3
  570.1 418.4 all-reduce.5
